TPU v7x, 32 devices: a whole 2x2x4 slice. The times are simulated.
32 devices in a mesh: rep: 4 (over x, core), fsdp: 8 (over z, y).
Axes of the slice: x: 2, y: 2, z: 4, core: 2. Of those that a mesh axis runs over, the one named last changes fastest.
Arguments:
- base_params: bfloat16 [14336, 8192], P(None, 'fsdp'), may hold values from -6 to 6
- local_params: bfloat16 [4, 14336, 8192], P('rep', None, 'fsdp'), may hold values from -6 to 6
- momentum: float32 [14336, 8192], P(('rep', 'fsdp')), may hold values from -4 to 4
Outputs:
- new_params: bfloat16 [14336, 8192], P(None, 'fsdp')
All inputs are finite; a program needn't handle non-finite values.
Results may differ from a plain program's by a relative error of at most 0.0077.
Values may be sent and summed in bfloat16 or wider, within the bound.
A program may use at most 512 MiB of HBM per device.

v0:
```python
import jax
import jax.numpy as jnp
from jax import lax
from jax.sharding import PartitionSpec as P

epsilon = 1e-06
code_max = 448.0
outer_rate = 0.7
nesterov = 0.9


def block_encode(tensor):
    dims = tensor.shape
    blocks = tensor.reshape(dims[:-1] + (dims[-1] // 128, 128))
    largest = jnp.max(jnp.abs(blocks), axis=-1)
    scales = ((largest + epsilon) / code_max).astype(jnp.bfloat16)
    scales = lax.optimization_barrier(scales)
    symbols = (blocks / scales.astype(jnp.float32)[..., None]).astype(jnp.bfloat16)
    return (symbols.reshape(dims), scales)


def decode_pieces(symbols, scales):
    lead = symbols.shape[0]
    row_count = symbols.shape[1]
    block_count = symbols.shape[2] // 128
    blocks = symbols.reshape(lead, row_count, block_count, 128).astype(jnp.float32)
    factor = jnp.swapaxes(scales, 1, 2).astype(jnp.float32)
    return blocks * factor[..., None]


def local(base_params, local_params, momentum):
    replicas = lax.axis_size("rep")
    groups = lax.axis_size("fsdp")
    owners = replicas * groups
    row_count = momentum.shape[0]
    col_count = base_params.shape[1]
    total_rows = base_params.shape[0]
    block_count = col_count // 128
    start = base_params.astype(jnp.float32)
    symbols, scales = block_encode(start - local_params[0].astype(jnp.float32))
    send_symbols = symbols.reshape(owners, row_count, col_count)
    send_scales = jnp.swapaxes(scales.reshape(owners, row_count, block_count), 1, 2)
    got_symbols, got_scales = (
        lax.all_to_all(send_symbols, ("rep", "fsdp"), split_axis=0, concat_axis=0, tiled=True),
        lax.all_to_all(send_scales, ("rep", "fsdp"), split_axis=0, concat_axis=0, tiled=True),
    )
    values = decode_pieces(got_symbols, got_scales)
    summed = jnp.sum(values.reshape(replicas, groups, row_count, block_count, 128), axis=0)
    outer_grad = (
        jnp.transpose(summed, (1, 0, 2, 3)).reshape(row_count, groups * col_count) / replicas
    )
    moment_next = nesterov * momentum + outer_grad
    update = outer_rate * (outer_grad + nesterov * moment_next)
    update_symbols, update_scales = block_encode(update)
    piece_symbols = jnp.transpose(update_symbols.reshape(row_count, groups, col_count), (1, 0, 2))
    piece_scales = jnp.transpose(update_scales.reshape(row_count, groups, block_count), (1, 2, 0))
    out_symbols = jnp.broadcast_to(
        piece_symbols[None], (replicas, groups, row_count, col_count)
    ).reshape(owners, row_count, col_count)
    out_scales = jnp.broadcast_to(
        piece_scales[None], (replicas, groups, block_count, row_count)
    ).reshape(owners, block_count, row_count)
    back_symbols, back_scales = (
        lax.all_to_all(out_symbols, ("rep", "fsdp"), split_axis=0, concat_axis=0, tiled=True),
        lax.all_to_all(out_scales, ("rep", "fsdp"), split_axis=0, concat_axis=0, tiled=True),
    )
    decoded = decode_pieces(back_symbols, back_scales).reshape(total_rows, col_count)
    return (start - decoded).astype(jnp.bfloat16)


def solution(mesh):
    return jax.shard_map(
        local,
        mesh=mesh,
        in_specs=(P(None, "fsdp"), P("rep", None, "fsdp"), P(("rep", "fsdp"), None)),
        out_specs=P(None, "fsdp"),
        check_vma=False,
    )
```

profile of v0, /device:TPU:0, one launch (start us, length us, event | category | flops | bytes accessed | tf_op | source)
XLA Modules:
  0.0 1875.5 jit_solution(8821600945241099387)
XLA Ops:
  0.0 56.4 %abs_bitcast_fusion = (f32[1792,8,8,128]{3,1,2,0:T(8,128)}, f32[14336,1024]{1,0:T(8,128)}) fusion(bf16[1,14336,1024]{2,1,0:T(8,128)(2,1)} %param.4, bf16[14336,1024]{1,0:T(8,128)(2,1)} %param.3), kind=kLoop, calls=%fused_computation.6 | loop fusion | flops 58720256 | bytes 176160768
  56.4 39.8 %copy.35 = f32[1792,8,8,128]{3,2,1,0:T(8,128)} copy(f32[1792,8,8,128]{3,1,2,0:T(8,128)} %get-tuple-element.7) | data formatting | bytes 117440512
  96.1 29.5 %reduce_max.18 = f32[14336,8]{1,0:T(8,128)} reduce(f32[14336,8,128]{2,1,0:T(8,128)} %bitcast.59, f32[]{:T(128)} %constant.7.clone.1), dimensions={2}, to_apply=%region_0.0 | reduce | flops 14565376 | bytes 59179012 | tf_op jit(solution)/shard_map/reduce_max | solution.py:15
  132.0 7.3 all-to-all-start.1
  143.3 22.8 %div.46 = f32[14336,8,128]{2,1,0:T(8,128)} broadcast(f32[14336,8]{1,0:T(8,128)} %copy.28), dimensions={0,1} | broadcast | bytes 59179008 | tf_op jit(solution)/shard_map/div | solution.py:18
  166.1 61.6 %div.47 = f32[32,448,1024]{2,1,0:T(8,128)} reshape(f32[14336,8,128]{2,1,0:T(8,128)} %div.46) | data formatting | bytes 117440512 | tf_op jit(solution)/shard_map/div | solution.py:18
  227.7 46.6 %divide_convert_fusion = bf16[32,448,1024]{2,1,0:T(8,128)(2,1)} fusion(f32[32,448,1024]{2,1,0:T(8,128)} %bitcast.62, f32[32,448,1024]{2,1,0:T(8,128)} %div.47), kind=kLoop, calls=%fused_computation.5 | loop fusion | flops 29360128 | bytes 146800640 | tf_op jit(solution)/shard_map/convert_element_type | solution.py:18
  285.3 648.4 %all-to-all-done = bf16[32,448,1024]{2,1,0:T(8,128)(2,1)} async-done(((bf16[32,448,1024]{2,1,0:T(8,128)(2,1)}), bf16[32,448,1024]{2,1,0:T(8,128)(2,1)}, u32[]{:S(2)}, u32[]{:S(2)}) %all-to-all-start) | async-done | bytes 29360160 | tf_op jit(solution)/shard_map/all_to_all | solution.py:44
  933.8 28.4 %copy.36 = f32[1792,8,8,128]{3,2,1,0:T(8,128)} copy(bf16[1792,8,8,128]{3,1,2,0:T(8,128)(2,1)} %bitcast.56) | data formatting | bytes 88080384
  962.2 27.3 %multiply_reduce_fusion = f32[8,448,8,128]{3,2,1,0:T(8,128)} fusion(f32[4,8,448,8,128]{4,3,2,1,0:T(8,128)} %bitcast.60, f32[4,8,448,8]{3,2,1,0:T(8,128)} %copy.30), kind=kLoop, calls=%fused_computation.4 | loop fusion | flops 25690112 | bytes 73859072 | tf_op jit(solution)/shard_map/reduce_sum | solution.py:48
  989.5 11.7 multiply_bitcast_fusion
  1001.2 12.5 copy.31
  1013.7 25.9 %abs_bitcast_fusion.1 = (f32[56,8,64,128]{3,1,2,0:T(8,128)}, f32[448,8192]{1,0:T(8,128)}) fusion(f32[448,8192]{1,0:T(8,128)} %param.5, f32[56,8,64,128]{3,2,1,0:T(8,128)} %bitcast.65), kind=kLoop, calls=%fused_computation.13 | loop fusion | flops 22020096 | bytes 58720256
  1039.5 13.6 copy.39
  1053.1 9.0 reduce_max.19
  1065.6 7.7 div.55
  1073.3 16.0 div.56
  1089.3 26.6 %copy.38 = f32[56,8,8,1024]{3,2,1,0:T(8,128)} copy(f32[56,8,8,1024]{3,1,2,0:T(8,128)} %bitcast.64) | data formatting | bytes 29360128
  1115.9 10.4 fusion.1
  1126.3 7.1 copy.32
  1133.4 11.9 broadcast_in_dim.4
  1155.7 649.8 %all-to-all-done.2 = bf16[32,448,1024]{2,1,0:T(8,128)(2,1)} async-done(((bf16[32,448,1024]{2,1,0:T(8,128)(2,1)}), bf16[32,448,1024]{2,1,0:T(8,128)(2,1)}, u32[]{:S(2)}, u32[]{:S(2)}) %all-to-all-start.2) | async-done | bytes 29360160 | tf_op jit(solution)/shard_map/all_to_all | solution.py:64
  1805.5 22.8 %mul.44 = f32[32,448,8,128]{3,2,1,0:T(8,128)} broadcast(f32[32,448,8]{2,1,0:T(8,128)} %copy.34), dimensions={0,1,2} | broadcast | bytes 59179008 | tf_op jit(solution)/shard_map/mul | solution.py:28
  1828.3 46.8 %fusion = bf16[14336,1024]{1,0:T(8,128)(2,1)} fusion(bf16[14336,1024]{1,0:T(8,128)(2,1)} %param.3, f32[1792,8,8,128]{3,2,1,0:T(8,128)} %bitcast.61, bf16[32,448,1024]{2,1,0:T(8,128)(2,1)} %all-to-all-done.2), kind=kLoop, calls=%fused_computation.2 | loop fusion | flops 73400320 | bytes 146800640 | tf_op jit(solution)/shard_map/convert_element_type | solution.py:68
  (17 shorter events, 35.1 us)
Async XLA Ops:
  132.0 142.3 %all-to-all-start.1 = ((bf16[32,8,448]{2,1,0:T(8,128)(2,1)}), bf16[32,8,448]{2,1,0:T(8,128)(2,1)S(1)}, u32[]{:S(2)}, u32[]{:S(2)}) async-start(bf16[32,8,448]{2,1,0:T(8,128)(2,1)} %copy.29), calls=%async_computation.1 | async-start | bytes 524288 | tf_op jit(solution)/shard_map/all_to_all | solution.py:45
  274.3 659.4 %all-to-all-start = ((bf16[32,448,1024]{2,1,0:T(8,128)(2,1)}), bf16[32,448,1024]{2,1,0:T(8,128)(2,1)}, u32[]{:S(2)}, u32[]{:S(2)}) async-start(bf16[32,448,1024]{2,1,0:T(8,128)(2,1)} %divide_convert_fusion), calls=%async_computation | async-start | bytes 58720256 | tf_op jit(solution)/shard_map/all_to_all | solution.py:44
  1063.1 70.4 %all-to-all-start.3 = ((bf16[32,8,448]{2,1,0:T(8,128)(2,1)}), bf16[32,8,448]{2,1,0:T(8,128)(2,1)S(1)}, u32[]{:S(2)}, u32[]{:S(2)}) async-start(bf16[32,8,448]{2,1,0:T(8,128)(2,1)} %bitcast.11), calls=%async_computation.3 | async-start | bytes 524288 | tf_op jit(solution)/shard_map/all_to_all | solution.py:65
  1145.3 660.2 %all-to-all-start.2 = ((bf16[32,448,1024]{2,1,0:T(8,128)(2,1)}), bf16[32,448,1024]{2,1,0:T(8,128)(2,1)}, u32[]{:S(2)}, u32[]{:S(2)}) async-start(bf16[32,448,1024]{2,1,0:T(8,128)(2,1)} %bitcast.63), calls=%async_computation.2 | async-start | bytes 58720256 | tf_op jit(solution)/shard_map/all_to_all | solution.py:64
where the time goes:
time: 1880 us
  waiting for transfers between devices  1300 us (69%)
  local copies, waits for them, and re-layouts  291 us (15%)
  other arithmetic  264 us (14%)
  starting transfers between devices  22.2 us (1%)
    all_to_all x1, waiting for transfers between devices, local(): lax.all_to_all(out_symbols, ('rep', 'fsdp'), split_axis=0, concat_axis=0,...  650 us
    all_to_all x1, waiting for transfers between devices, local(): lax.all_to_all(send_symbols, ('rep', 'fsdp'), split_axis=0, concat_axis=0...  648 us
    unnamed x4, local copies, waits for them, and re-layouts  108 us
    div x4, local copies, waits for them, and re-layouts, block_encode(): blocks / scales.astype(jnp.float32)[..., None]  108 us
    unnamed x2, other arithmetic  82.2 us
    convert_element_type x2, other arithmetic, block_encode(): (blocks / scales.astype(jnp.float32)[..., None]).astype(jnp.bfloat16)  57 us
    convert_element_type x1, other arithmetic, local(): return (start - decoded).astype(jnp.bfloat16)  46.8 us
    reduce_max x2, other arithmetic, block_encode(): largest = jnp.max(jnp.abs(blocks), axis=-1)  38.5 us
  transfers between devices with their start and end apart: 4, of which 2 were waited for; matrix products, arithmetic and copies ran while one was open for 11% of the time, Pallas kernels for 0%

commit v1 on v0

v1 whole, which is shorter than its diff:
```python
import functools

import jax
import jax.numpy as jnp
from jax import lax
from jax.experimental import pallas as pl
from jax.experimental.pallas import tpu as pltpu
from jax.sharding import PartitionSpec as P

epsilon = 1e-06
code_max = 448.0
outer_rate = 0.7
nesterov = 0.9

BLOCK = 128
GROUP = 16
MESH = pl.DeviceIdType.MESH

LAG_PAIR = 1
LAG_OWN = 4
LAG_PASS = 7
SLOTS = 4


def round_trip(values):
    largest = jnp.max(jnp.abs(values), axis=-1, keepdims=True)
    scales = ((largest + epsilon) / code_max).astype(jnp.bfloat16).astype(jnp.float32)
    symbols = (values * (1.0 / scales)).astype(jnp.bfloat16)
    return symbols.astype(jnp.float32) * scales


def kernel(
    rep_count, fsdp_count, chunk, base, loc, mom, out,
    base_buf, loc_buf, mom_buf, mom_out, sib_out, pair_out, new_out,
    sib_in, pair_in, mom_in,
    base_sem, loc_sem, mom_sem,
    mom_send, sib_send, pair_send, new_send, pass_send,
    sib_recv, pair_recv, mom_recv, new_recv, far_recv,
):
    r = lax.axis_index("rep")
    f = lax.axis_index("fsdp")
    x = lax.div(r, 2)
    c = lax.rem(r, 2)
    sibling = (2 * x + 1 - c, f)
    across = (2 * (1 - x) + c, f)
    cols = base.shape[1]
    quarter_rows = base.shape[0] // rep_count
    own_rows = mom.shape[0]
    per_piece = own_rows // chunk
    chunks = quarter_rows // chunk
    quarters = (2 * (1 - x) + 1 - c, 2 * x + 1 - c, 2 * (1 - x) + c, 2 * x + c)
    lags = (0, 0, LAG_PAIR, LAG_OWN)

    barrier = pltpu.get_barrier_semaphore()
    pl.semaphore_signal(barrier, inc=1, device_id=sibling, device_id_type=MESH)
    pl.semaphore_signal(barrier, inc=1, device_id=across, device_id_type=MESH)

    def greet(j, carry):
        peer = lax.rem(f + j, fsdp_count)
        pl.semaphore_signal(barrier, inc=1, device_id=(r, peer), device_id_type=MESH)
        return carry

    lax.fori_loop(1, fsdp_count, greet, 0)

    def rows_of(k, quarter):
        piece = lax.rem(f + lax.div(k, per_piece), fsdp_count)
        start = quarter * quarter_rows + piece * own_rows + lax.rem(k, per_piece) * chunk
        return pl.ds(pl.multiple_of(start, 16), chunk)

    def mom_peer(k):
        return lax.rem(f + fsdp_count - lax.div(k, per_piece), fsdp_count)

    def loads(i, k):
        slot = lax.rem(k, 2)
        rows = rows_of(k, quarters[i])
        return (
            pltpu.make_async_copy(base.at[rows, :], base_buf.at[slot, i], base_sem.at[slot, i]),
            pltpu.make_async_copy(loc.at[0, rows, :], loc_buf.at[slot, i], loc_sem.at[slot, i]),
        )

    def mom_load(k):
        slot = lax.rem(k, 2)
        start = pl.multiple_of(lax.rem(k, per_piece) * chunk, 16)
        first = pl.multiple_of(mom_peer(k) * cols, BLOCK)
        return pltpu.make_async_copy(
            mom.at[pl.ds(start, chunk), pl.ds(first, cols)], mom_buf.at[slot], mom_sem.at[slot]
        )

    def remote(src, dst, send, recv, device):
        return pltpu.make_async_remote_copy(
            src_ref=src, dst_ref=dst, send_sem=send, recv_sem=recv,
            device_id=device, device_id_type=MESH,
        )

    def mom_copy(k):
        slot = lax.rem(k, SLOTS)
        return remote(
            mom_out.at[slot], mom_in.at[k], mom_send.at[slot], mom_recv.at[k], (r, mom_peer(k))
        )

    def sib_copy(i, k):
        slot = lax.rem(k, SLOTS)
        return remote(
            sib_out.at[slot, i], sib_in.at[k, i], sib_send.at[slot, i], sib_recv.at[k, i], sibling
        )

    def pair_copy(k):
        slot = lax.rem(k, SLOTS)
        return remote(
            pair_out.at[slot], pair_in.at[k], pair_send.at[slot], pair_recv.at[k], across
        )

    def new_copies(k):
        slot = lax.rem(k, SLOTS)
        src = new_out.at[slot]
        dst = out.at[rows_of(k, quarters[3]), :]
        return (
            remote(src, dst, new_send.at[slot, 0], new_recv.at[k], across),
            remote(src, dst, new_send.at[slot, 1], far_recv.at[0], sibling),
            pltpu.make_async_copy(src, dst, new_send.at[slot, 2]),
        )

    def pass_copy(rows):
        return remote(out.at[rows, :], out.at[rows, :], pass_send, far_recv.at[1], sibling)

    def active(k):
        return jnp.logical_and(k >= 0, k < chunks)

    def prefetch(step):
        @pl.when(active(step))
        def _():
            mom_load(step).start()

        for i in range(4):
            k = step - lags[i]

            @pl.when(active(k))
            def _(i=i, k=k):
                for copy in loads(i, k):
                    copy.start()

    def each_block(body):
        def group(g, carry):
            rows = pl.ds(pl.multiple_of(g * GROUP, GROUP), GROUP)
            for b in range(cols // BLOCK):
                body(rows, pl.ds(b * BLOCK, BLOCK))
            return carry

        lax.fori_loop(0, chunk // GROUP, group, 0)

    def change(i, slot, rows, block):
        start = base_buf[slot, i, rows, block].astype(jnp.float32)
        return start, round_trip(start - loc_buf[slot, i, rows, block].astype(jnp.float32))

    def send_momentum(k):
        slot = lax.rem(k, 2)
        mom_load(k).wait()

        @pl.when(k < per_piece)
        def _():
            def body(rows, block):
                mom_in[k, rows, block] = mom_buf[slot, rows, block].astype(jnp.bfloat16)

            each_block(body)

        @pl.when(k >= per_piece)
        def _():
            @pl.when(k >= per_piece + SLOTS)
            def _():
                mom_copy(k - SLOTS).wait_send()

            to = lax.rem(k, SLOTS)

            def body(rows, block):
                mom_out[to, rows, block] = mom_buf[slot, rows, block].astype(jnp.bfloat16)

            each_block(body)
            mom_copy(k).start()

    def send_sibling(k):
        slot = lax.rem(k, 2)
        to = lax.rem(k, SLOTS)
        for i in range(2):
            for copy in loads(i, k):
                copy.wait()

            @pl.when(k >= SLOTS)
            def _(i=i):
                sib_copy(i, k - SLOTS).wait_send()

            def body(rows, block, i=i):
                sib_out[to, i, rows, block] = change(i, slot, rows, block)[1].astype(jnp.bfloat16)

            each_block(body)
            sib_copy(i, k).start()

    def send_pair(k):
        slot = lax.rem(k, 2)
        to = lax.rem(k, SLOTS)
        for copy in loads(2, k):
            copy.wait()

        @pl.when(k >= SLOTS)
        def _():
            pair_copy(k - SLOTS).wait_send()

        sib_copy(0, k).wait_recv()

        def body(rows, block):
            total = change(2, slot, rows, block)[1] + sib_in[k, 0, rows, block].astype(jnp.float32)
            pair_out[to, rows, block] = total.astype(jnp.bfloat16)

        each_block(body)
        pair_copy(k).start()

    def step_own(k):
        slot = lax.rem(k, 2)
        to = lax.rem(k, SLOTS)
        for copy in loads(3, k):
            copy.wait()

        @pl.when(k >= SLOTS)
        def _():
            first, second, third = new_copies(k - SLOTS)
            first.wait_send()
            second.wait_send()
            third.wait()

        sib_copy(1, k).wait_recv()

        @pl.when(k >= per_piece)
        def _():
            mom_copy(k).wait_recv()

        pair_copy(k).wait_recv()

        def body(rows, block):
            start, mine = change(3, slot, rows, block)
            total = mine + sib_in[k, 1, rows, block].astype(jnp.float32)
            total = total + pair_in[k, rows, block].astype(jnp.float32)
            outer_grad = total / rep_count
            moment_next = nesterov * mom_in[k, rows, block].astype(jnp.float32) + outer_grad
            update = outer_rate * (outer_grad + nesterov * moment_next)
            new_out[to, rows, block] = (start - round_trip(update)).astype(jnp.bfloat16)

        each_block(body)
        for copy in new_copies(k):
            copy.start()

    def pass_on(k):
        rows = rows_of(k, quarters[2])
        remote(
            out.at[rows, :], out.at[rows, :], pass_send, new_recv.at[k], across
        ).wait_recv()
        pass_copy(rows).start()

    prefetch(0)
    pl.semaphore_wait(barrier, fsdp_count + 1)

    def step(s, carry):
        prefetch(s + 1)
        for lag, stage in (
            (0, send_sibling),
            (LAG_PAIR, send_pair),
            (0, send_momentum),
            (LAG_OWN, step_own),
            (LAG_PASS, pass_on),
        ):
            k = s - lag

            @pl.when(active(k))
            def _(stage=stage, k=k):
                stage(k)

        return carry

    lax.fori_loop(0, chunks + LAG_PASS, step, 0)

    def drain(k, carry):
        mom_copy(k).wait_send()
        sib_copy(0, k).wait_send()
        sib_copy(1, k).wait_send()
        pair_copy(k).wait_send()
        first, second, third = new_copies(k)
        first.wait_send()
        second.wait_send()
        third.wait()
        return carry

    lax.fori_loop(chunks - SLOTS, chunks, drain, 0)

    def quarter_of(index):
        return pl.ds(pl.multiple_of(index * quarter_rows, 16), quarter_rows)

    pass_copy(quarter_of(quarters[2])).wait_send()
    for i in range(2):
        rows = quarter_of(quarters[1 - i])
        remote(out.at[rows, :], out.at[rows, :], pass_send, far_recv.at[i], sibling).wait_recv()


def chunk_rows(own_rows):
    best = GROUP
    for size in range(GROUP, 113, GROUP):
        if own_rows % size == 0:
            best = size
    return best


def local(base_params, local_params, momentum):
    rep_count = lax.axis_size("rep")
    fsdp_count = lax.axis_size("fsdp")
    total_rows, cols = base_params.shape
    chunk = chunk_rows(momentum.shape[0])
    chunks = total_rows // rep_count // chunk
    bf16, f32 = jnp.bfloat16, jnp.float32
    dma = pltpu.SemaphoreType.DMA
    anywhere = pl.BlockSpec(memory_space=pl.ANY)
    return pl.pallas_call(
        functools.partial(kernel, rep_count, fsdp_count, chunk),
        out_shape=jax.ShapeDtypeStruct((total_rows, cols), bf16),
        in_specs=[anywhere] * 3,
        out_specs=anywhere,
        scratch_shapes=[
            pltpu.VMEM((2, 4, chunk, cols), bf16),
            pltpu.VMEM((2, 4, chunk, cols), bf16),
            pltpu.VMEM((2, chunk, cols), f32),
            pltpu.VMEM((SLOTS, chunk, cols), bf16),
            pltpu.VMEM((SLOTS, 2, chunk, cols), bf16),
            pltpu.VMEM((SLOTS, chunk, cols), bf16),
            pltpu.VMEM((SLOTS, chunk, cols), bf16),
            pltpu.VMEM((chunks, 2, chunk, cols), bf16),
            pltpu.VMEM((chunks, chunk, cols), bf16),
            pltpu.VMEM((chunks, chunk, cols), bf16),
            dma((2, 4)),
            dma((2, 4)),
            dma((2,)),
            dma((SLOTS,)),
            dma((SLOTS, 2)),
            dma((SLOTS,)),
            dma((SLOTS, 3)),
            dma,
            dma((chunks, 2)),
            dma((chunks,)),
            dma((chunks,)),
            dma((chunks,)),
            dma((2,)),
        ],
        compiler_params=pltpu.CompilerParams(
            collective_id=0, has_side_effects=True, vmem_limit_bytes=56 * 1024 * 1024
        ),
    )(base_params, local_params, momentum)


def solution(mesh):
    return jax.shard_map(
        local,
        mesh=mesh,
        in_specs=(P(None, "fsdp"), P("rep", None, "fsdp"), P(("rep", "fsdp"), None)),
        out_specs=P(None, "fsdp"),
        check_vma=False,
    )
```

time: 1880 us -> 351 us (0.19)
  waiting for transfers between devices: 1300 us -> 0 us
  Pallas kernels: 0 us -> 330 us
  local copies, waits for them, and re-layouts: 291 us -> 20.2 us
  other arithmetic: 264 us -> 0 us
  starting transfers between devices: 22.2 us -> 0 us
    all_to_all x4 -> x0, waiting for transfers between devices: 1300 us -> none  [the longest x1 650 us: local(): lax.all_to_all(out_symbols, ('rep', 'fsdp'), split_axis=0, concat_axis=0,...]
    pallas_call x0 -> x1, Pallas kernels: none -> 330 us  [local(): pl.pallas_call(functools.partial(kernel, rep_count, fsdp_count, chunk), o...]
    div x5 -> x0, local copies, waits for them, and re-layouts: 121 us -> none  [the longest x4 108 us: block_encode(): blocks / scales.astype(jnp.float32)[..., None]]
    convert_element_type x6 -> x0, other arithmetic: 104 us -> none  [the longest x2 57 us: block_encode(): (blocks / scales.astype(jnp.float32)[..., None]).astype(jnp.bfloat16)]
    unnamed x4 -> x1, local copies, waits for them, and re-layouts: 108 us -> 20.2 us
    unnamed x2 -> x0, other arithmetic: 82.2 us -> none
    reduce_max x2 -> x0, other arithmetic: 38.5 us -> none  [block_encode(): largest = jnp.max(jnp.abs(blocks), axis=-1)]
    reduce_sum x1 -> x0, other arithmetic: 27.3 us -> none  [local(): jnp.sum(values.reshape(replicas, groups, row_count, block_count, 128), ax...]
  transfers between devices with their start and end apart: 4 -> 0, of which waited for: 2 -> 0; matrix products, arithmetic and copies ran while one was open for 11% -> 0% of each run, Pallas kernels for 0% -> 0%
where the time goes in v1:
time: 351 us; the launch traced here: 350 us
  Pallas kernels  330 us (94%)
  local copies, waits for them, and re-layouts  20.2 us (6%)
    pallas_call x1, Pallas kernels, local(): pl.pallas_call(functools.partial(kernel, rep_count, fsdp_count, chunk), o...  330 us
    unnamed x1, local copies, waits for them, and re-layouts  20.2 us

profile of v1, /device:TPU:0, one launch (start us, length us, event | category | flops | bytes accessed | tf_op | source)
XLA Modules:
  0.0 350.4 jit_solution(11080224180539709728)
XLA Ops:
  0.0 330.2 %shard_map.37 = bf16[14336,1024]{1,0:T(8,128)(2,1)} custom-call(bf16[14336,1024]{1,0:T(8,128)(2,1)} %base.1, bf16[1,14336,1024]{2,1,0:T(8,128)(2,1)} %loc.1, f32[448,8192]{1,0:T(8,128)} %mom.1), custom_call_target="tpu_custom_call" | custom-call | tf_op jit(solution)/shard_map/pallas_call | solution.py:318
  330.2 20.2 %copy.5 = bf16[14336,1024]{1,0:T(8,128)(2,1)} copy(bf16[14336,1024]{1,0:T(8,128)(2,1)} %shard_map.37) | data formatting | bytes 58720256

commit v2 on v1

--- a/solution.py
+++ b/solution.py
@@ -20,6 +20,8 @@
 LAG_OWN = 4
 LAG_PASS = 7
 SLOTS = 4
+PARTS = 8
+RING = 10
 
 
 def round_trip(values):
@@ -35,7 +37,7 @@
     sib_in, pair_in, mom_in,
     base_sem, loc_sem, mom_sem,
     mom_send, sib_send, pair_send, new_send, pass_send,
-    sib_recv, pair_recv, mom_recv, new_recv, far_recv,
+    sib_recv, pair_recv, mom_recv, new_recv, far_recv, sib_free, pair_free,
 ):
     r = lax.axis_index("rep")
     f = lax.axis_index("fsdp")
@@ -101,13 +103,15 @@
     def sib_copy(i, k):
         slot = lax.rem(k, SLOTS)
         return remote(
-            sib_out.at[slot, i], sib_in.at[k, i], sib_send.at[slot, i], sib_recv.at[k, i], sibling
+            sib_out.at[slot, i], sib_in.at[lax.rem(k, RING), i], sib_send.at[slot, i],
+            sib_recv.at[lax.rem(k, RING), i], sibling,
         )
 
     def pair_copy(k):
         slot = lax.rem(k, SLOTS)
         return remote(
-            pair_out.at[slot], pair_in.at[k], pair_send.at[slot], pair_recv.at[k], across
+            pair_out.at[slot], pair_in.at[lax.rem(k, RING)], pair_send.at[slot],
+            pair_recv.at[lax.rem(k, RING)], across,
         )
 
     def new_copies(k):
@@ -180,6 +184,11 @@
     def send_sibling(k):
         slot = lax.rem(k, 2)
         to = lax.rem(k, SLOTS)
+
+        @pl.when(k >= RING)
+        def _():
+            pl.semaphore_wait(sib_free, 1)
+
         for i in range(2):
             for copy in loads(i, k):
                 copy.wait()
@@ -204,10 +213,14 @@
         def _():
             pair_copy(k - SLOTS).wait_send()
 
+        @pl.when(k >= RING)
+        def _():
+            pl.semaphore_wait(pair_free, 1)
+
         sib_copy(0, k).wait_recv()
 
         def body(rows, block):
-            total = change(2, slot, rows, block)[1] + sib_in[k, 0, rows, block].astype(jnp.float32)
+            total = change(2, slot, rows, block)[1] + sib_in[lax.rem(k, RING), 0, rows, block].astype(jnp.float32)
             pair_out[to, rows, block] = total.astype(jnp.bfloat16)
 
         each_block(body)
@@ -236,8 +249,8 @@
 
         def body(rows, block):
             start, mine = change(3, slot, rows, block)
-            total = mine + sib_in[k, 1, rows, block].astype(jnp.float32)
-            total = total + pair_in[k, rows, block].astype(jnp.float32)
+            total = mine + sib_in[lax.rem(k, RING), 1, rows, block].astype(jnp.float32)
+            total = total + pair_in[lax.rem(k, RING), rows, block].astype(jnp.float32)
             outer_grad = total / rep_count
             moment_next = nesterov * mom_in[k, rows, block].astype(jnp.float32) + outer_grad
             update = outer_rate * (outer_grad + nesterov * moment_next)
@@ -246,6 +259,11 @@
         each_block(body)
         for copy in new_copies(k):
             copy.start()
+
+        @pl.when(k < chunks - RING)
+        def _():
+            pl.semaphore_signal(sib_free, inc=1, device_id=sibling, device_id_type=MESH)
+            pl.semaphore_signal(pair_free, inc=1, device_id=across, device_id_type=MESH)
 
     def pass_on(k):
         rows = rows_of(k, quarters[2])
@@ -298,12 +316,24 @@
         remote(out.at[rows, :], out.at[rows, :], pass_send, far_recv.at[i], sibling).wait_recv()
 
 
+def write_kernel(rows, src, dst, sem):
+    copies = [
+        pltpu.make_async_copy(
+            src.at[pl.ds(p * rows, rows), :], dst.at[pl.ds(p * rows, rows), :], sem.at[p]
+        )
+        for p in range(PARTS)
+    ]
+    for copy in copies:
+        copy.start()
+    for copy in copies:
+        copy.wait()
+
+
 def chunk_rows(own_rows):
-    best = GROUP
-    for size in range(GROUP, 113, GROUP):
+    for size in (64, 80, 96, 112, 128, 48, 32):
         if own_rows % size == 0:
-            best = size
-    return best
+            return size
+    return GROUP
 
 
 def local(base_params, local_params, momentum):
@@ -315,9 +345,9 @@
     bf16, f32 = jnp.bfloat16, jnp.float32
     dma = pltpu.SemaphoreType.DMA
     anywhere = pl.BlockSpec(memory_space=pl.ANY)
-    return pl.pallas_call(
+    gathered = pl.pallas_call(
         functools.partial(kernel, rep_count, fsdp_count, chunk),
-        out_shape=jax.ShapeDtypeStruct((total_rows, cols), bf16),
+        out_shape=pltpu.VMEM((total_rows, cols), bf16),
         in_specs=[anywhere] * 3,
         out_specs=anywhere,
         scratch_shapes=[
@@ -328,8 +358,8 @@
             pltpu.VMEM((SLOTS, 2, chunk, cols), bf16),
             pltpu.VMEM((SLOTS, chunk, cols), bf16),
             pltpu.VMEM((SLOTS, chunk, cols), bf16),
-            pltpu.VMEM((chunks, 2, chunk, cols), bf16),
-            pltpu.VMEM((chunks, chunk, cols), bf16),
+            pltpu.VMEM((RING, 2, chunk, cols), bf16),
+            pltpu.VMEM((RING, chunk, cols), bf16),
             pltpu.VMEM((chunks, chunk, cols), bf16),
             dma((2, 4)),
             dma((2, 4)),
@@ -339,16 +369,26 @@
             dma((SLOTS,)),
             dma((SLOTS, 3)),
             dma,
-            dma((chunks, 2)),
-            dma((chunks,)),
+            dma((RING, 2)),
+            dma((RING,)),
             dma((chunks,)),
             dma((chunks,)),
             dma((2,)),
+            pltpu.SemaphoreType.REGULAR,
+            pltpu.SemaphoreType.REGULAR,
         ],
         compiler_params=pltpu.CompilerParams(
-            collective_id=0, has_side_effects=True, vmem_limit_bytes=56 * 1024 * 1024
+            collective_id=0, has_side_effects=True, vmem_limit_bytes=24 * 1024 * 1024
         ),
     )(base_params, local_params, momentum)
+    return pl.pallas_call(
+        functools.partial(write_kernel, total_rows // PARTS),
+        out_shape=jax.ShapeDtypeStruct((total_rows, cols), bf16),
+        in_specs=[anywhere],
+        out_specs=anywhere,
+        scratch_shapes=[dma((PARTS,))],
+        compiler_params=pltpu.CompilerParams(vmem_limit_bytes=1024 * 1024),
+    )(gathered)
 
 
 def solution(mesh):

time: 351 us -> 338 us (0.963)
  local copies, waits for them, and re-layouts: 20.2 us -> 0 us
  Pallas kernels: 330 us -> 338 us
    unnamed x1 -> x0, local copies, waits for them, and re-layouts: 20.2 us -> none
    pallas_call x0 -> x1, Pallas kernels: none -> 9.84 us  [local(): pl.pallas_call(functools.partial(write_kernel, total_rows // PARTS), out_...]
where the time goes in v2:
time: 338 us
  Pallas kernels  338 us (100%)
    pallas_call x1, Pallas kernels, local(): pl.pallas_call(functools.partial(kernel, rep_count, fsdp_count, chunk), o...  328 us
    pallas_call x1, Pallas kernels, local(): pl.pallas_call(functools.partial(write_kernel, total_rows // PARTS), out_...  9.84 us

profile of v2, /device:TPU:0, one launch (start us, length us, event | category | flops | bytes accessed | tf_op | source)
XLA Modules:
  0.0 337.8 jit_solution(1504643709001586955)
XLA Ops:
  0.0 327.9 %shard_map.37.src = bf16[14336,1024]{1,0:T(8,128)(2,1)S(1)} custom-call(bf16[14336,1024]{1,0:T(8,128)(2,1)} %base.1, bf16[1,14336,1024]{2,1,0:T(8,128)(2,1)} %loc.1, f32[448,8192]{1,0:T(8,128)} %mom.1), custom_call_target="tpu_custom_call" | custom-call | tf_op jit(solution)/shard_map/pallas_call | solution.py:348
  327.9 9.8 %shard_map.38 = bf16[14336,1024]{1,0:T(8,128)(2,1)} custom-call(bf16[14336,1024]{1,0:T(8,128)(2,1)S(1)} %shard_map.37.src), custom_call_target="tpu_custom_call" | custom-call | tf_op jit(solution)/shard_map/pallas_call | solution.py:384

commit v3 on v2

--- a/solution.py
+++ b/solution.py
@@ -16,9 +16,10 @@
 GROUP = 16
 MESH = pl.DeviceIdType.MESH
 
-LAG_PAIR = 1
-LAG_OWN = 4
-LAG_PASS = 7
+LAG_ENCODE = -1
+LAG_PAIR = 0
+LAG_OWN = 3
+LAG_PASS = 6
 SLOTS = 4
 PARTS = 8
 RING = 10
@@ -51,7 +52,7 @@
     per_piece = own_rows // chunk
     chunks = quarter_rows // chunk
     quarters = (2 * (1 - x) + 1 - c, 2 * x + 1 - c, 2 * (1 - x) + c, 2 * x + c)
-    lags = (0, 0, LAG_PAIR, LAG_OWN)
+    lags = (LAG_ENCODE, LAG_ENCODE, LAG_PAIR, LAG_OWN)
 
     barrier = pltpu.get_barrier_semaphore()
     pl.semaphore_signal(barrier, inc=1, device_id=sibling, device_id_type=MESH)
@@ -182,13 +183,16 @@
             mom_copy(k).start()
 
     def send_sibling(k):
+        @pl.when(k >= RING)
+        def _():
+            pl.semaphore_wait(sib_free, 1)
+
+        for i in range(2):
+            sib_copy(i, k).start()
+
+    def encode_sibling(k):
         slot = lax.rem(k, 2)
         to = lax.rem(k, SLOTS)
-
-        @pl.when(k >= RING)
-        def _():
-            pl.semaphore_wait(sib_free, 1)
-
         for i in range(2):
             for copy in loads(i, k):
                 copy.wait()
@@ -201,7 +205,6 @@
                 sib_out[to, i, rows, block] = change(i, slot, rows, block)[1].astype(jnp.bfloat16)
 
             each_block(body)
-            sib_copy(i, k).start()
 
     def send_pair(k):
         slot = lax.rem(k, 2)
@@ -272,16 +275,19 @@
         ).wait_recv()
         pass_copy(rows).start()
 
-    prefetch(0)
+    prefetch(jnp.int32(-1))
+    prefetch(jnp.int32(0))
+    encode_sibling(jnp.int32(0))
     pl.semaphore_wait(barrier, fsdp_count + 1)
 
     def step(s, carry):
         prefetch(s + 1)
         for lag, stage in (
             (0, send_sibling),
+            (LAG_ENCODE, encode_sibling),
             (LAG_PAIR, send_pair),
+            (LAG_OWN, step_own),
             (0, send_momentum),
-            (LAG_OWN, step_own),
             (LAG_PASS, pass_on),
         ):
             k = s - lag

time: 338 us -> 337 us (level)
  no operation moved by 1% of the time
where the time goes in v3:
time: 337 us
  Pallas kernels  337 us (100%)
    pallas_call x1, Pallas kernels, local(): pl.pallas_call(functools.partial(kernel, rep_count, fsdp_count, chunk), o...  327 us
    pallas_call x1, Pallas kernels, local(): pl.pallas_call(functools.partial(write_kernel, total_rows // PARTS), out_...  9.84 us

profile of v3, /device:TPU:0, one launch (start us, length us, event | category | flops | bytes accessed | tf_op | source)
XLA Modules:
  0.0 337.3 jit_solution(15899954086251631338)
XLA Ops:
  0.0 327.5 %shard_map.37.src = bf16[14336,1024]{1,0:T(8,128)(2,1)S(1)} custom-call(bf16[14336,1024]{1,0:T(8,128)(2,1)} %base.1, bf16[1,14336,1024]{2,1,0:T(8,128)(2,1)} %loc.1, f32[448,8192]{1,0:T(8,128)} %mom.1), custom_call_target="tpu_custom_call" | custom-call | tf_op jit(solution)/shard_map/pallas_call | solution.py:354
  327.5 9.8 %shard_map.38 = bf16[14336,1024]{1,0:T(8,128)(2,1)} custom-call(bf16[14336,1024]{1,0:T(8,128)(2,1)S(1)} %shard_map.37.src), custom_call_target="tpu_custom_call" | custom-call | tf_op jit(solution)/shard_map/pallas_call | solution.py:390
